TPU v7x, 512 devices: a whole 4x8x8 slice. The times are simulated.
512 devices in a mesh: dp: 64 (over x, z, core), tensor: 8 (over y).
Axes of the slice: x: 4, y: 8, z: 8, core: 2. Of those that a mesh axis runs over, the one named last changes fastest.
Arguments:
- queries: bfloat16 [28672, 6144], P('dp', 'tensor'), may hold values from -6 to 6
- keys_in: bfloat16 [28672, 6144], P('dp', 'tensor'), may hold values from -6 to 6
- values: bfloat16 [28672, 6144], P('dp', 'tensor'), may hold values from -6 to 6
- q_gain: float32 [128], replicated, may hold values from 0.5 to 6
- k_gain: float32 [128], replicated, may hold values from 0.5 to 6
- cotangent: bfloat16 [16384, 6144], P(('dp', 'tensor')), may hold values from -6 to 6
- patch_counts: int32 [64, 6], replicated, may hold values from 0 to 240, as said below
- image_owner: int32 [64, 6], replicated, may hold values from 0 to 63, as said below
- pack_offset: int32 [64, 6], replicated, may hold values from 0 to 256, as said below
Outputs:
- attn_out: bfloat16 [16384, 6144], P(('dp', 'tensor'))
- grad_q: bfloat16 [28672, 6144], P('dp', 'tensor')
- grad_k: bfloat16 [28672, 6144], P('dp', 'tensor')
- grad_v: bfloat16 [28672, 6144], P('dp', 'tensor')
Inputs may be any that keep to these rules, and one draw needn't show every extreme that they name: `patch_counts`: counts are multiples of 16; 0 marks an empty entry. The counts of one device sum to at most 448, reached on some device in every draw; the largest single image is reached in every draw. `image_owner`: an image's owner is the device itself or one of its two neighbours on the cycle (dp index plus or minus one modulo 64); of each device's 6 entries two stay, two go to each neighbour. The images that one device sends to one neighbour hold at most 96 patches in all, reached in every draw. `pack_offset`: the nonempty images owned by a device tile its 256 rows exactly.
All inputs are finite; a program needn't handle non-finite values.
Results may differ from a plain program's by a relative error of at most 0.029.
The roundings to bfloat16 on the way count: a program that leaves them out, or rounds other values in their place, can miss the bound.
Values may be sent and summed in bfloat16 or wider, within the bound.
A program may use at most 64 MiB of HBM per device.

v0:
```python
import jax
import jax.numpy as jnp
from jax import lax
from jax.sharding import PartitionSpec as P

OWN_ROWS = 256
CAP = 96
SRC_ROWS = 448


EPS = 1e-06


def padded(x, sides, width):
    for axis, dim in sides:
        peers, length = (lax.axis_size(axis), x.shape[dim])
        up = [(i, (i + 1) % peers) for i in range(peers)]
        down = [(j, i) for i, j in up]
        last = lax.slice_in_dim(x, length - width, length, axis=dim)
        leading = lax.slice_in_dim(x, 0, width, axis=dim)
        before = lax.ppermute(last, axis, up)
        after = lax.ppermute(leading, axis, down)
        x = jnp.concatenate([before, x, after], axis=dim)
    return x


def normalize(entries):
    centre = jnp.mean(entries, axis=-1, keepdims=True)
    centred = entries - centre
    variance = jnp.mean(centred * centred, axis=-1, keepdims=True)
    inverse = lax.rsqrt(variance + EPS)
    return (centred * inverse, inverse)


def norm_back(grad_norm, normed, inverse, gain):
    scaled = grad_norm * gain
    first = jnp.mean(scaled, axis=-1, keepdims=True)
    second = jnp.mean(scaled * normed, axis=-1, keepdims=True)
    return inverse * (scaled - first - normed * second)


def attend(queries, keys_in, values, cotangent, segment, q_gain, k_gain):
    row_count = queries.shape[0]
    head_size = q_gain.shape[0]
    head_count = queries.shape[1] // head_size
    shaped = (row_count, head_count, head_size)
    query_hat, query_inv = normalize(queries.reshape(shaped).astype(jnp.float32))
    key_hat, key_inv = normalize(keys_in.reshape(shaped).astype(jnp.float32))
    query_norm = (query_hat * q_gain).astype(jnp.bfloat16)
    key_norm = (key_hat * k_gain).astype(jnp.bfloat16)
    value_rows = values.reshape(shaped)
    cot_rows = cotangent.reshape(shaped)
    score_scale = head_size ** (-0.5)
    scores = (
        jnp.einsum("qhd,khd->hqk", query_norm, key_norm, preferred_element_type=jnp.float32)
        * score_scale
    )
    same_image = segment[:, None] == segment[None, :]
    scores = jnp.where(same_image[None], scores, -1e30)
    row_max = jnp.max(scores, axis=2, keepdims=True)
    powers = jnp.exp(scores - row_max)
    weights = powers / jnp.sum(powers, axis=2, keepdims=True)
    weights_low = weights.astype(jnp.bfloat16)
    output = jnp.einsum(
        "hqk,khd->qhd", weights_low, value_rows, preferred_element_type=jnp.float32
    ).astype(jnp.bfloat16)
    grad_weights = jnp.einsum(
        "qhd,khd->hqk", cot_rows, value_rows, preferred_element_type=jnp.float32
    )
    row_inner = jnp.sum(weights * grad_weights, axis=2, keepdims=True)
    grad_scores = (weights * (grad_weights - row_inner) * score_scale).astype(jnp.bfloat16)
    grad_v = jnp.einsum(
        "hqk,qhd->khd", weights_low, cot_rows, preferred_element_type=jnp.float32
    ).astype(jnp.bfloat16)
    grad_qnorm = jnp.einsum(
        "hqk,khd->qhd", grad_scores, key_norm, preferred_element_type=jnp.float32
    )
    grad_knorm = jnp.einsum(
        "hqk,qhd->khd", grad_scores, query_norm, preferred_element_type=jnp.float32
    )
    grad_q = norm_back(grad_qnorm, query_hat, query_inv, q_gain).astype(jnp.bfloat16)
    grad_k = norm_back(grad_knorm, key_hat, key_inv, k_gain).astype(jnp.bfloat16)
    flat_shape = (row_count, head_count * head_size)
    return (
        output.reshape(flat_shape),
        grad_q.reshape(flat_shape),
        grad_k.reshape(flat_shape),
        grad_v.reshape(flat_shape),
    )


def table_row(table, source):
    return lax.dynamic_index_in_dim(table, source, 0, keepdims=False)


def source_entries(tables, source):
    counts = table_row(tables[0], source)
    owners = table_row(tables[1], source)
    offsets = table_row(tables[2], source)
    starts = jnp.cumsum(counts) - counts
    return (counts, owners, offsets, starts)


def slot_begins(counts, owners, wanted):
    chosen = owners == wanted
    lengths = jnp.where(chosen, counts, 0)
    return (chosen, jnp.cumsum(lengths) - lengths)


def slot_rows(entries, wanted, length):
    counts, owners, offsets, starts = entries
    chosen, begins = slot_begins(counts, owners, wanted)
    position = jnp.arange(length, dtype=jnp.int32)[:, None]
    matches = chosen[None] & (position >= begins[None]) & (position < (begins + counts)[None])
    usable = jnp.any(matches, axis=1)
    within = position[:, 0] - jnp.sum(jnp.where(matches, begins[None], 0), axis=1)
    source_row = jnp.sum(jnp.where(matches, starts[None], 0), axis=1) + within
    target_row = jnp.sum(jnp.where(matches, offsets[None], 0), axis=1) + within
    return (jnp.where(usable, source_row, 0), jnp.where(usable, target_row, 0), usable)


def pick_rows(array, picked, usable, axis_dim):
    taken = jnp.take(array, picked, axis=axis_dim)
    mask_shape = [1] * taken.ndim
    mask_shape[axis_dim] = picked.shape[0]
    return jnp.where(usable.reshape(mask_shape), taken, jnp.zeros((), array.dtype))


def owner_index(tables, my_index, cycle_size):
    from_left = source_entries(tables, (my_index - 1) % cycle_size)
    own_entries = source_entries(tables, my_index)
    from_right = source_entries(tables, (my_index + 1) % cycle_size)
    chosen_left, begins_left = slot_begins(from_left[0], from_left[1], my_index)
    chosen_right, begins_right = slot_begins(from_right[0], from_right[1], my_index)
    chosen = jnp.concatenate([chosen_left, own_entries[1] == my_index, chosen_right])
    offsets = jnp.concatenate([from_left[2], own_entries[2], from_right[2]])
    counts = jnp.concatenate([from_left[0], own_entries[0], from_right[0]])
    base_index = jnp.concatenate([begins_left, CAP + own_entries[3], CAP + SRC_ROWS + begins_right])
    position = jnp.arange(OWN_ROWS, dtype=jnp.int32)[:, None]
    matches = chosen[None] & (position >= offsets[None]) & (position < (offsets + counts)[None])
    gather_row = (
        jnp.sum(jnp.where(matches, (base_index - offsets)[None], 0), axis=1) + position[:, 0]
    )
    labels = jnp.arange(counts.shape[0], dtype=jnp.int32)
    segment = jnp.sum(jnp.where(matches, labels[None], 0), axis=1)
    return (gather_row, segment)


def source_index(tables, my_index, cycle_size):
    leftward = (my_index - 1) % cycle_size
    rightward = (my_index + 1) % cycle_size
    counts, owners, offsets, starts = source_entries(tables, my_index)
    _, begins_left = slot_begins(counts, owners, leftward)
    _, begins_right = slot_begins(counts, owners, rightward)
    base_index = jnp.where(
        owners == my_index,
        CAP + offsets,
        jnp.where(owners == leftward, begins_left, CAP + OWN_ROWS + begins_right),
    )
    position = jnp.arange(SRC_ROWS, dtype=jnp.int32)[:, None]
    matches = (position >= starts[None]) & (position < (starts + counts)[None])
    in_use = jnp.any(matches, axis=1)
    within = position[:, 0] - jnp.sum(jnp.where(matches, starts[None], 0), axis=1)
    gather_row = jnp.where(
        in_use, jnp.sum(jnp.where(matches, base_index[None], 0), axis=1) + within, 0
    )
    labels = jnp.arange(counts.shape[0], dtype=jnp.int32)
    segment = jnp.where(in_use, jnp.sum(jnp.where(matches, labels[None], 0), axis=1), -1)
    return (gather_row, segment, in_use)


def send_rows(stacked, tables, my_index, cycle_size, axis_dim):
    entries = source_entries(tables, my_index)
    left_rows, _, left_ok = slot_rows(entries, (my_index - 1) % cycle_size, CAP)
    right_rows, _, right_ok = slot_rows(entries, (my_index + 1) % cycle_size, CAP)
    return jnp.concatenate(
        [
            pick_rows(stacked, left_rows, left_ok, axis_dim),
            pick_rows(stacked, right_rows, right_ok, axis_dim),
        ],
        axis=axis_dim,
    )


def return_rows(stacked, tables, my_index, cycle_size, axis_dim):
    _, left_rows, left_ok = slot_rows(
        source_entries(tables, (my_index - 1) % cycle_size), my_index, CAP
    )
    _, right_rows, right_ok = slot_rows(
        source_entries(tables, (my_index + 1) % cycle_size), my_index, CAP
    )
    return jnp.concatenate(
        [
            pick_rows(stacked, left_rows, left_ok, axis_dim),
            pick_rows(stacked, right_rows, right_ok, axis_dim),
        ],
        axis=axis_dim,
    )


def edge_rows(extended, axis_dim):
    first = lax.slice_in_dim(extended, 0, CAP, axis=axis_dim)
    last = lax.slice_in_dim(extended, 3 * CAP, 4 * CAP, axis=axis_dim)
    return (first, last)


def per_device(
    queries, keys_in, values, q_gain, k_gain, cotangent, patch_counts, image_owner, pack_offset
):
    cycle_size = lax.axis_size("dp")
    my_index = lax.axis_index("dp")
    tables = (patch_counts, image_owner, pack_offset)
    own_rows, own_segment = owner_index(tables, my_index, cycle_size)
    src_rows, src_segment, in_use = source_index(tables, my_index, cycle_size)
    cot_heads = lax.all_to_all(cotangent, "tensor", split_axis=1, concat_axis=0, tiled=True)
    returning = return_rows(cot_heads, tables, my_index, cycle_size, 0)
    arrived = padded(returning, (("dp", 0),), CAP)
    back_left, back_right = edge_rows(arrived, 0)
    cot_source = pick_rows(
        jnp.concatenate([back_left, cot_heads, back_right], axis=0), src_rows, in_use, 0
    )
    source_out, grad_q, grad_k, grad_v = attend(
        queries, keys_in, values, cot_source, src_segment, q_gain, k_gain
    )
    zero_value = jnp.zeros((), jnp.bfloat16)
    grad_q = jnp.where(in_use[:, None], grad_q, zero_value)
    grad_k = jnp.where(in_use[:, None], grad_k, zero_value)
    grad_v = jnp.where(in_use[:, None], grad_v, zero_value)
    outgoing = send_rows(source_out, tables, my_index, cycle_size, 0)
    extended = padded(outgoing, (("dp", 0),), CAP)
    from_left, from_right = edge_rows(extended, 0)
    owned_out = jnp.take(
        jnp.concatenate([from_left, source_out, from_right], axis=0), own_rows, axis=0
    )
    attn_out = lax.all_to_all(owned_out, "tensor", split_axis=0, concat_axis=1, tiled=True)
    return (attn_out, grad_q, grad_k, grad_v)


def solution(mesh):
    in_specs = (
        P("dp", "tensor"),
        P("dp", "tensor"),
        P("dp", "tensor"),
        P(),
        P(),
        P(("dp", "tensor"), None),
        P(),
        P(),
        P(),
    )
    out_specs = (P(("dp", "tensor"), None), P("dp", "tensor"), P("dp", "tensor"), P("dp", "tensor"))
    return jax.shard_map(
        per_device, mesh=mesh, in_specs=in_specs, out_specs=out_specs, check_vma=False
    )
```

profile of v0, /device:TPU:8, one launch (start us, length us, event | category | flops | bytes accessed | tf_op | source)
XLA Modules:
  0.0 164.1 jit_solution(1129494299206326346)
XLA Ops:
  0.7 2.5 %copy.67 = f32[448,768]{0,1:T(8,128)} copy(bf16[448,768]{1,0:T(8,128)(2,1)} %param.14) | data formatting | bytes 2064384 | tf_op jit(solution)/shard_map/convert_element_type | solution.py:48
  3.2 1.9 %copy.68 = f32[448,6,128]{2,0,1:T(8,128)S(1)} copy(f32[448,6,128]{0,2,1:T(8,128)} %bitcast.94) | data formatting | bytes 2752512 | tf_op jit(solution)/shard_map/convert_element_type | solution.py:48
  5.1 2.1 %reduce_sum.211 = f32[448,6]{0,1:T(8,128)S(1)} reduce(f32[448,6,128]{0,2,1:T(8,128)} %bitcast.95, f32[]{:T(128)} %constant.166.clone.1), dimensions={2}, to_apply=%region_10.11 | reduce | flops 341376 | bytes 1387012 | tf_op jit(solution)/shard_map/reduce_sum | solution.py:28
  7.2 1.4 copy.65
  8.6 1.9 %copy.66 = f32[448,6,128]{2,0,1:T(8,128)S(1)} copy(f32[448,6,128]{0,2,1:T(8,128)} %bitcast.92) | data formatting | bytes 2752512 | tf_op jit(solution)/shard_map/convert_element_type | solution.py:47
  10.5 2.2 %reduce_sum.209 = f32[448,6]{0,1:T(8,128)} reduce(f32[448,6,128]{0,2,1:T(8,128)} %bitcast.93, f32[]{:T(128)} %constant.166.clone.1), dimensions={2}, to_apply=%region_8.9 | reduce | flops 341376 | bytes 1387012 | tf_op jit(solution)/shard_map/reduce_sum | solution.py:28
  14.1 1.5 constant_dynamic-slice_fusion.2
  16.9 1.5 constant_dynamic-slice_fusion.6
  26.1 2.1 %dynamic-slice_reduce_fusion.1 = (s32[6]{0:T(128)}, s32[6]{0:T(128)}, s32[1,6]{0,1:T(8,128)}) fusion(s32[64,6]{0,1:T(8,128)} %param.21, s32[]{:T(128)S(6)} %select_n.282, s32[]{:T(128)S(6)} %select_n.285, s32[]{:T(128)S(6)} %select_n.283), kind=kLoop, calls=%fused_computation.110 | loop fusion | bytes 156 | tf_op jit(solution)/shard_map/jit(dynamic_index_in_dim)/dynamic_slice | solution.py:93
  35.6 2.8 %multiply_convert_fusion.3 = (bf16[448,6,128]{2,0,1:T(8,128)(2,1)}, bf16[448,6,128]{2,0,1:T(8,128)(2,1)}) fusion(f32[448,6,128]{2,0,1:T(8,128)S(1)} %copy.68, f32[128]{0:T(128)S(1)} %copy-done.39, f32[448,6]{0,1:T(8,128)S(1)} %add_rsqrt_fusion, f32[448,6]{0,1:T(8,128)S(1)} %broadcast_multiply_fusion.4, f32[128]{0:T(128)S(1)} %copy-done.40, ...), kind=kLoop, calls=%fused_computation.34 | loop fusion | flops 2752512 | bytes 4172800 | tf_op jit(solution)/shard_map/convert_element_type | solution.py:50
  38.4 5.8 %fusion.83 = (f32[6,448]{1,0:T(8,128)S(1)}, f32[6,448,448]{1,2,0:T(8,128)}) fusion(pred[448,448]{0,1:T(8,128)(4,1)} %broadcast_compare_fusion, bf16[448,6,128]{2,0,1:T(8,128)(2,1)} %get-tuple-element.81, bf16[448,6,128]{2,0,1:T(8,128)(2,1)} %get-tuple-element.80), kind=kOutput, calls=%fused_computation.182 | convolution fusion | flops 313098688 | bytes 6404608 | tf_op jit(solution)/shard_map/sub | solution.py:61
  44.9 3.7 %fusion.42 = bf16[448,6,128]{2,0,1:T(8,128)(2,1)S(1)} fusion(bf16[448,6,128]{0,2,1:T(8,128)(2,1)S(1)} %bitcast.97, f32[6,448,448]{1,2,0:T(8,128)} %get-tuple-element.73, f32[6,448]{1,0:T(8,128)S(1)} %get-tuple-element.72), kind=kOutput, calls=%fused_computation.43 | convolution fusion | flops 311033856 | bytes 6203904 | tf_op jit(solution)/shard_map/hqk,khd->qhd/dot_general | solution.py:64
  50.4 12.6 %collective-permute-start.1 = (bf16[96,768]{1,0:T(8,128)(2,1)S(1)}, bf16[96,768]{1,0:T(8,128)(2,1)S(1)}, u32[]{:S(2)}, u32[]{:S(2)}) collective-permute-start(bf16[96,768]{1,0:T(8,128)(2,1)S(1)} %select_select_fusion.5), channel_id=1, source_target_pairs={{8,0},{16,8},{24,16},{32,24},{40,32},{48,40},{56,48},{64,56},{72,6... | collective-permute-start | bytes 442376 | tf_op jit(solution)/shard_map/ppermute | solution.py:22
  64.1 1.9 %collective-permute-start = (bf16[96,768]{1,0:T(8,128)(2,1)S(1)}, bf16[96,768]{1,0:T(8,128)(2,1)}, u32[]{:S(2)}, u32[]{:S(2)}) collective-permute-start(bf16[96,768]{1,0:T(8,128)(2,1)S(1)} %select_select_fusion.6), channel_id=1, source_target_pairs={{0,8},{8,16},{16,24},{24,32},{32,40},{40,48},{48,56},{56,64},{64,7... | collective-permute-start | bytes 442376 | tf_op jit(solution)/shard_map/ppermute | solution.py:21
  66.8 7.5 %all-to-all-start.1 = ((bf16[32,8,768]{2,0,1:T(8,128)(2,1)}), bf16[32,8,768]{2,0,1:T(8,128)(2,1)S(1)}, u32[]{:S(2)}, u32[]{:S(2)}) async-start(bf16[32,8,768]{2,0,1:T(8,128)(2,1)} %bitcast.88), calls=%async_computation.1 | async-start | bytes 786432 | tf_op jit(solution)/shard_map/all_to_all | solution.py:215
  79.5 5.3 %all-to-all-done.1 = bf16[32,8,768]{2,0,1:T(8,128)(2,1)S(1)} async-done(((bf16[32,8,768]{2,0,1:T(8,128)(2,1)}), bf16[32,8,768]{2,0,1:T(8,128)(2,1)S(1)}, u32[]{:S(2)}, u32[]{:S(2)}) %all-to-all-start.1) | async-done | bytes 393248 | tf_op jit(solution)/shard_map/all_to_all | solution.py:215
  85.7 6.6 %collective-permute-start.3 = (bf16[96,768]{1,0:T(8,128)(2,1)S(1)}, bf16[96,768]{1,0:T(8,128)(2,1)S(1)}, u32[]{:S(2)}, u32[]{:S(2)}) collective-permute-start(bf16[96,768]{1,0:T(8,128)(2,1)S(1)} %select_select_fusion.3), channel_id=1, source_target_pairs={{8,0},{16,8},{24,16},{32,24},{40,32},{48,40},{56,48},{64,56},{72,6... | collective-permute-start | bytes 442376 | tf_op jit(solution)/shard_map/ppermute | solution.py:22
  93.2 1.9 %collective-permute-start.2 = (bf16[96,768]{1,0:T(8,128)(2,1)S(1)}, bf16[96,768]{1,0:T(8,128)(2,1)S(1)}, u32[]{:S(2)}, u32[]{:S(2)}) collective-permute-start(bf16[96,768]{1,0:T(8,128)(2,1)S(1)} %select_select_fusion.4), channel_id=1, source_target_pairs={{0,8},{8,16},{16,24},{24,32},{32,40},{40,48},{48,56},{56,64},{64,7... | collective-permute-start | bytes 442376 | tf_op jit(solution)/shard_map/ppermute | solution.py:21
  96.0 5.5 %all-to-all-start = ((bf16[8,32,768]{2,1,0:T(8,128)(2,1)}), bf16[8,32,768]{2,1,0:T(8,128)(2,1)}, u32[]{:S(2)}, u32[]{:S(2)}) async-start(bf16[8,32,768]{2,1,0:T(8,128)(2,1)} %broadcast_select_fusion), calls=%async_computation | async-start | bytes 786432 | tf_op jit(solution)/shard_map/all_to_all | solution.py:235
  101.4 1.5 collective-permute-done.2
  103.0 2.1 %gather_fusion.1 = bf16[448,768]{1,0:T(8,128)(2,1)S(1)} fusion(bf16[448,768]{1,0:T(8,128)(2,1)S(1)} %pad_maximum_fusion.1, s32[1024]{0:T(1024)S(1)} %pad_clamp_fusion), kind=kCustom, calls=%fused_computation.5 | custom fusion | bytes 1378048 | tf_op jit(solution)/shard_map/jit(_take)/gather | solution.py:123
  106.3 4.6 %fusion.45 = f32[6,448,448]{1,2,0:T(8,128)} fusion(bf16[448,6,128]{0,2,1:T(8,128)(2,1)S(1)} %bitcast.98, bf16[448,6,128]{0,2,1:T(8,128)(2,1)} %bitcast.99, pred[448]{0:T(512)(128)(4,1)} %compare_and_fusion.5, pred[448]{0:T(512)(128)(4,1)} %copy-done.22), kind=kOutput, calls=%fused_computation.50 | convolution fusion | flops 308969472 | bytes 6194048 | tf_op jit(solution)/shard_map/qhd,khd->hqk/dot_general | solution.py:67
  110.9 12.1 %fusion.81 = (f32[448,6]{0,1:T(8,128)}, f32[448,6]{0,1:T(8,128)}, f32[448,6,128]{2,0,1:T(8,128)}) fusion(f32[448,6]{0,1:T(8,128)} %copy-done.11, f32[448,6,128]{2,0,1:T(8,128)S(1)} %copy-done.1, f32[448,6]{0,1:T(8,128)} %copy-done.8, f32[128]{0:T(128)} %param.17, bf16[448,6,128]{2,0,1:T(8,128)(2,1)} %get-tuple-element.81, f32[6,448,448]{1,2,0:T(8,128)} %fusion.45, ...), kind=kOutput, calls=%fused_computation.180 | convolution fusion | flops 318773056 | bytes 13128704 | tf_op jit(solution)/shard_map/hqk,qhd->khd/dot_general | solution.py:78
  123.1 12.9 %fusion.82 = (f32[448,6]{0,1:T(8,128)}, f32[448,6]{0,1:T(8,128)}, f32[448,6,128]{2,0,1:T(8,128)}) fusion(f32[448,6]{0,1:T(8,128)} %copy-done.9, f32[448,6,128]{2,0,1:T(8,128)S(1)} %copy.66, f32[448,6]{0,1:T(8,128)S(1)} %broadcast_multiply_fusion.5, f32[128]{0:T(128)} %param.16, bf16[448,6,128]{2,0,1:T(8,128)(2,1)} %get-tuple-element.80, ...), kind=kOutput, calls=%fused_computation.181 | convolution fusion | flops 318773056 | bytes 13128704 | tf_op jit(solution)/shard_map/hqk,khd->qhd/dot_general | solution.py:75
  136.0 4.3 %fusion.39 = bf16[448,6,128]{2,0,1:T(8,128)(2,1)} fusion(bf16[448,6,128]{0,2,1:T(8,128)(2,1)S(1)} %bitcast.100, pred[448]{0:T(512)(128)(4,1)} %compare_and_fusion.5, pred[448]{0:T(512)(128)(4,1)} %copy-done.22, f32[6,448,448]{1,2,0:T(8,128)} %get-tuple-element.73, f32[6,448]{1,0:T(8,128)} %copy-done.41), kind=kOutput, calls=%fused_computation.42 | convolution fusion | flops 311721984 | bytes 6204800 | tf_op jit(solution)/shard_map/hqk,qhd->khd/dot_general | solution.py:72
  140.3 1.8 %copy.103 = bf16[8,4,8,768]{3,2,0,1:T(8,128)(2,1)} copy(bf16[8,4,8,768]{3,2,1,0:T(8,128)(2,1)} %bitcast.48) | data formatting | bytes 786432 | tf_op jit(solution)/shard_map/all_to_all | solution.py:235
  144.9 4.2 %multiply_convert_fusion.1 = bf16[448,6,128]{2,0,1:T(8,128)(2,1)} fusion(f32[448,6,128]{2,0,1:T(8,128)} %get-tuple-element.74, f32[448,6,128]{2,0,1:T(8,128)S(1)} %copy-done.1, f32[448,6]{0,1:T(8,128)S(1)} %broadcast_multiply_fusion, f32[448,6]{0,1:T(8,128)S(1)} %broadcast_multiply_fusion.1, f32[448,6]{0,1:T(8,128)} %copy-done.11, f32[448,6]{0,1:T(8,128)} %copy-done.8), kind=kLoop, calls=%fused_computation.26 | loop fusion | flops 2408448 | bytes 3483648 | tf_op jit(solution)/shard_map/convert_element_type | solution.py:82
  149.1 1.4 copy.83
  150.6 4.2 %multiply_convert_fusion.2 = bf16[448,6,128]{2,0,1:T(8,128)(2,1)} fusion(f32[448,6,128]{2,0,1:T(8,128)} %get-tuple-element.75, f32[448,6,128]{2,0,1:T(8,128)S(1)} %copy.66, f32[448,6]{0,1:T(8,128)S(1)} %broadcast_multiply_fusion.2, f32[448,6]{0,1:T(8,128)S(1)} %broadcast_multiply_fusion.3, f32[448,6]{0,1:T(8,128)S(1)} %copy-done.10, ...), kind=kLoop, calls=%fused_computation.28 | loop fusion | flops 2408448 | bytes 3483648 | tf_op jit(solution)/shard_map/convert_element_type | solution.py:81
  154.8 2.2 %copy.82 = bf16[448,6,128]{0,2,1:T(8,128)(2,1)} copy(bf16[448,6,128]{2,0,1:T(8,128)(2,1)} %multiply_convert_fusion.2) | data formatting | bytes 1376256 | tf_op jit(solution)/shard_map/convert_element_type | solution.py:81
  157.0 2.6 %bitcast_select_fusion = (bf16[448,768]{0,1:T(8,128)(2,1)S(1)}, bf16[448,768]{0,1:T(8,128)(2,1)}, bf16[448,768]{0,1:T(8,128)(2,1)}) fusion(bf16[448,6,128]{0,2,1:T(8,128)(2,1)S(1)} %copy.85, pred[448]{0:T(512)(128)(4,1)S(1)} %copy-done.24, bf16[448,6,128]{0,2,1:T(8,128)(2,1)S(1)} %copy.83, bf16[448,6,128]{0,2,1:T(8,128)(2,1)} %copy.82), kind=kLoop, calls=%fused_computation.45 | loop fusion | flops 1032192 | bytes 4129216 | tf_op jit(solution)/shard_map/jit(_where)/select_n | solution.py:228
  159.6 2.3 %copy.86 = bf16[448,768]{1,0:T(8,128)(2,1)} copy(bf16[448,768]{0,1:T(8,128)(2,1)} %get-tuple-element.66) | data formatting | bytes 1376256
  (167 shorter events, 35.7 us)
Async XLA Ops:
  5.1 30.5 %copy-start = (f32[448,6,128]{2,0,1:T(8,128)}, f32[448,6,128]{2,0,1:T(8,128)S(1)}, u32[]{:S(2)}) copy-start(f32[448,6,128]{2,0,1:T(8,128)S(1)} %copy.68) | copy-start | bytes 4128772
  5.1 2.1 %copy-start.6 = (bf16[448,768]{1,0:T(8,128)(2,1)S(1)}, bf16[448,768]{1,0:T(8,128)(2,1)}, u32[]{:S(2)}) copy-start(bf16[448,768]{1,0:T(8,128)(2,1)} %param.13) | copy-start | bytes 2064388
  14.1 30.2 %copy-start.3 = (bf16[448,768]{0,1:T(8,128)(2,1)}, bf16[448,768]{0,1:T(8,128)(2,1)S(1)}, u32[]{:S(2)}) copy-start(bf16[448,768]{0,1:T(8,128)(2,1)S(1)} %copy.69) | copy-start | bytes 2064388
  29.5 5.1 %copy-start.13 = (f32[448,6]{0,1:T(8,128)S(1)}, f32[448,6]{0,1:T(8,128)}, u32[]{:S(2)}) copy-start(f32[448,6]{0,1:T(8,128)} %reduce_sum.209) | copy-start | bytes 32260
  30.8 2.0 %copy-start.35 = (s32[6]{0:T(128)}, s32[6]{0:T(128)S(1)}, u32[]{:S(2)}) copy-start(s32[6]{0:T(128)S(1)} %get-tuple-element.62) | copy-start | bytes 76
  33.8 1.8 %copy-start.40 = (f32[128]{0:T(128)S(1)}, f32[128]{0:T(128)}, u32[]{:S(2)}) copy-start(f32[128]{0:T(128)} %param.16) | copy-start | bytes 1540
  34.7 3.8 %copy-start.11 = (f32[448,6]{0,1:T(8,128)}, f32[448,6]{0,1:T(8,128)S(1)}, u32[]{:S(2)}) copy-start(f32[448,6]{0,1:T(8,128)S(1)} %add_rsqrt_fusion) | copy-start | bytes 32260
  35.6 2.8 %copy-start.9 = (f32[448,6]{0,1:T(8,128)}, f32[448,6]{0,1:T(8,128)S(1)}, u32[]{:S(2)}) copy-start(f32[448,6]{0,1:T(8,128)S(1)} %add_rsqrt_fusion.1) | copy-start | bytes 32260
  49.5 16.6 %copy-start.7 = (bf16[32,6144]{1,0:T(8,128)(2,1)S(1)}, bf16[32,6144]{1,0:T(8,128)(2,1)}, u32[]{:S(2)}) copy-start(bf16[32,6144]{1,0:T(8,128)(2,1)} %param.18) | copy-start | bytes 1179652
  50.4 26.3 %collective-permute-start.1 = (bf16[96,768]{1,0:T(8,128)(2,1)S(1)}, bf16[96,768]{1,0:T(8,128)(2,1)S(1)}, u32[]{:S(2)}, u32[]{:S(2)}) collective-permute-start(bf16[96,768]{1,0:T(8,128)(2,1)S(1)} %select_select_fusion.5), channel_id=1, source_target_pairs={{8,0},{16,8},{24,16},{32,24},{40,32},{48,40},{56,48},{64,56},{72,6... | collective-permute-start | bytes 442376 | tf_op jit(solution)/shard_map/ppermute | solution.py:22
  63.1 11.3 %copy-start.17 = (s32[1,6]{0,1:T(8,128)S(1)}, s32[1,6]{0,1:T(8,128)}, u32[]{:S(2)}) copy-start(s32[1,6]{0,1:T(8,128)} %get-tuple-element.47) | copy-start | bytes 76
  63.1 11.4 %copy-start.16 = (s32[1,6]{0,1:T(8,128)S(1)}, s32[1,6]{0,1:T(8,128)}, u32[]{:S(2)}) copy-start(s32[1,6]{0,1:T(8,128)} %get-tuple-element.45) | copy-start | bytes 76
  63.1 11.5 %copy-start.19 = (s32[1,6]{0,1:T(8,128)S(1)}, s32[1,6]{0,1:T(8,128)}, u32[]{:S(2)}) copy-start(s32[1,6]{0,1:T(8,128)} %get-tuple-element.43) | copy-start | bytes 76
  63.1 11.5 %copy-start.18 = (s32[1,6]{0,1:T(8,128)S(1)}, s32[1,6]{0,1:T(8,128)}, u32[]{:S(2)}) copy-start(s32[1,6]{0,1:T(8,128)} %get-tuple-element.41) | copy-start | bytes 76
  63.1 12.1 %copy-start.27 = (s32[6]{0:T(128)S(1)}, s32[6]{0:T(128)}, u32[]{:S(2)}) copy-start(s32[6]{0:T(128)} %get-tuple-element.18) | copy-start | bytes 76
  63.1 12.2 %copy-start.38 = (pred[6]{0:T(512)(128)(4,1)S(1)}, pred[6]{0:T(512)(128)(4,1)}, u32[]{:S(2)}) copy-start(pred[6]{0:T(512)(128)(4,1)} %get-tuple-element.67) | copy-start | bytes 22
  63.2 12.4 %copy-start.28 = (s32[6]{0:T(128)S(1)}, s32[6]{0:T(128)}, u32[]{:S(2)}) copy-start(s32[6]{0:T(128)} %get-tuple-element.19) | copy-start | bytes 76
  63.2 12.4 %copy-start.25 = (s32[1,6]{1,0:T(1,128)S(1)}, s32[1,6]{1,0:T(1,128)}, u32[]{:S(2)}) copy-start(s32[1,6]{1,0:T(1,128)} %copy.100) | copy-start | bytes 76
  63.2 12.4 %copy-start.26 = (s32[1,6]{1,0:T(1,128)S(1)}, s32[1,6]{1,0:T(1,128)}, u32[]{:S(2)}) copy-start(s32[1,6]{1,0:T(1,128)} %copy.98) | copy-start | bytes 76
  63.2 12.5 %copy-start.37 = (s32[6]{0:T(128)S(1)}, s32[6]{0:T(128)}, u32[]{:S(2)}) copy-start(s32[6]{0:T(128)} %get-tuple-element.63) | copy-start | bytes 76
  63.2 12.8 %copy-start.14 = (s32[448]{0:T(512)S(1)}, s32[448]{0:T(512)}, u32[]{:S(2)}) copy-start(s32[448]{0:T(512)} %get-tuple-element.28) | copy-start | bytes 5380
  63.2 12.8 %copy-start.15 = (s32[448]{0:T(512)S(1)}, s32[448]{0:T(512)}, u32[]{:S(2)}) copy-start(s32[448]{0:T(512)} %get-tuple-element.30) | copy-start | bytes 5380
  63.2 12.8 %copy-start.23 = (pred[448]{0:T(512)(128)(4,1)S(1)}, pred[448]{0:T(512)(128)(4,1)}, u32[]{:S(2)}) copy-start(pred[448]{0:T(512)(128)(4,1)} %copy-done.22) | copy-start | bytes 1348
  64.1 13.2 %collective-permute-start = (bf16[96,768]{1,0:T(8,128)(2,1)S(1)}, bf16[96,768]{1,0:T(8,128)(2,1)}, u32[]{:S(2)}, u32[]{:S(2)}) collective-permute-start(bf16[96,768]{1,0:T(8,128)(2,1)S(1)} %select_select_fusion.6), channel_id=1, source_target_pairs={{0,8},{8,16},{16,24},{24,32},{32,40},{40,48},{48,56},{56,64},{64,7... | collective-permute-start | bytes 442376 | tf_op jit(solution)/shard_map/ppermute | solution.py:21
  66.8 18.0 %all-to-all-start.1 = ((bf16[32,8,768]{2,0,1:T(8,128)(2,1)}), bf16[32,8,768]{2,0,1:T(8,128)(2,1)S(1)}, u32[]{:S(2)}, u32[]{:S(2)}) async-start(bf16[32,8,768]{2,0,1:T(8,128)(2,1)} %bitcast.88), calls=%async_computation.1 | async-start | bytes 786432 | tf_op jit(solution)/shard_map/all_to_all | solution.py:215
  85.7 15.7 %collective-permute-start.3 = (bf16[96,768]{1,0:T(8,128)(2,1)S(1)}, bf16[96,768]{1,0:T(8,128)(2,1)S(1)}, u32[]{:S(2)}, u32[]{:S(2)}) collective-permute-start(bf16[96,768]{1,0:T(8,128)(2,1)S(1)} %select_select_fusion.3), channel_id=1, source_target_pairs={{8,0},{16,8},{24,16},{32,24},{40,32},{48,40},{56,48},{64,56},{72,6... | collective-permute-start | bytes 442376 | tf_op jit(solution)/shard_map/ppermute | solution.py:22
  93.2 9.8 %collective-permute-start.2 = (bf16[96,768]{1,0:T(8,128)(2,1)S(1)}, bf16[96,768]{1,0:T(8,128)(2,1)S(1)}, u32[]{:S(2)}, u32[]{:S(2)}) collective-permute-start(bf16[96,768]{1,0:T(8,128)(2,1)S(1)} %select_select_fusion.4), channel_id=1, source_target_pairs={{0,8},{8,16},{16,24},{24,32},{32,40},{40,48},{48,56},{56,64},{64,7... | collective-permute-start | bytes 442376 | tf_op jit(solution)/shard_map/ppermute | solution.py:21
  96.0 44.4 %all-to-all-start = ((bf16[8,32,768]{2,1,0:T(8,128)(2,1)}), bf16[8,32,768]{2,1,0:T(8,128)(2,1)}, u32[]{:S(2)}, u32[]{:S(2)}) async-start(bf16[8,32,768]{2,1,0:T(8,128)(2,1)} %broadcast_select_fusion), calls=%async_computation | async-start | bytes 786432 | tf_op jit(solution)/shard_map/all_to_all | solution.py:235
  106.3 4.6 %copy-start.1 = (f32[448,6,128]{2,0,1:T(8,128)S(1)}, f32[448,6,128]{2,0,1:T(8,128)}, u32[]{:S(2)}) copy-start(f32[448,6,128]{2,0,1:T(8,128)} %copy-done) | copy-start | bytes 4128772
  123.1 12.9 %copy-start.5 = (bf16[448,768]{0,1:T(8,128)(2,1)S(1)}, bf16[448,768]{0,1:T(8,128)(2,1)}, u32[]{:S(2)}) copy-start(bf16[448,768]{0,1:T(8,128)(2,1)} %copy.78) | copy-start | bytes 2064388
  154.8 2.3 %copy-start.24 = (pred[448]{0:T(512)(128)(4,1)S(1)}, pred[448]{0:T(512)(128)(4,1)}, u32[]{:S(2)}) copy-start(pred[448]{0:T(512)(128)(4,1)} %copy-done.22) | copy-start | bytes 1348
  159.6 2.3 %copy-start.2 = (bf16[448,768]{0,1:T(8,128)(2,1)S(1)}, bf16[448,768]{0,1:T(8,128)(2,1)}, u32[]{:S(2)}) copy-start(bf16[448,768]{0,1:T(8,128)(2,1)} %get-tuple-element.65) | copy-start | bytes 2064388
  (16 other events, 16.7 us)
where the time goes:
time: 166 us; the launch traced here: 164 us
  matrix products  43.5 us (26%)
  local copies, waits for them, and re-layouts  40.2 us (24%)
  other arithmetic  36.2 us (22%)
  starting transfers between devices  36 us (22%)
  waiting for transfers between devices  6.82 us (4%)
    ppermute x2, starting transfers between devices, padded(): after = lax.ppermute(leading, axis, down)  19.2 us
    dot_general x1, matrix products, attend(): jnp.einsum('hqk,khd->qhd', grad_scores, key_norm, preferred_element_type=...  12.9 us
    dot_general x1, matrix products, attend(): jnp.einsum('hqk,qhd->khd', grad_scores, query_norm, preferred_element_typ...  12.1 us
    unnamed x95, local copies, waits for them, and re-layouts  11.6 us
    all_to_all x1, starting transfers between devices, per_device(): lax.all_to_all(cotangent, 'tensor', split_axis=1, concat_axis=0, tiled=True)  7.54 us
    gather x6, local copies, waits for them, and re-layouts, pick_rows(): taken = jnp.take(array, picked, axis=axis_dim)  6.45 us
    sub x1, matrix products, attend(): powers = jnp.exp(scores - row_max)  5.82 us
    all_to_all x1, starting transfers between devices, per_device(): lax.all_to_all(owned_out, 'tensor', split_axis=0, concat_axis=1, tiled=True)  5.45 us
  transfers between devices with their start and end apart: 6, of which 2 were waited for; matrix products, arithmetic and copies ran while one was open for 28% of the time, Pallas kernels for 0%

commit v1 on v0

v1 whole, which is shorter than its diff:
```python
import functools

import jax
import jax.numpy as jnp
from jax import lax
from jax.experimental import pallas as pl
from jax.experimental.pallas import tpu as pltpu
from jax.sharding import PartitionSpec as P

MESH = pl.DeviceIdType.MESH
HD = 128
OWN_ROWS = 256
CAP = 96
SRC_ROWS = 448
ENTRIES = 6
BLOCK = 16
TILES = 2
TILE = SRC_ROWS // TILES
OWN_BLOCKS = OWN_ROWS // BLOCK
CAP_BLOCKS = CAP // BLOCK
SRC_BLOCKS = SRC_ROWS // BLOCK
TILE_BLOCKS = TILE // BLOCK
EPS = 1e-06
BF16 = jnp.bfloat16
F32 = jnp.float32


def begins_of(counts, owners, wanted):
    begins, total = [], jnp.int32(0)
    chosen = [owner == wanted for owner in owners]
    for count, mine in zip(counts, chosen):
        begins.append(total)
        total = total + jnp.where(mine, count, 0)
    return chosen, begins


def slot_source(chosen, begins, targets, block):
    shift = jnp.int32(0)
    for mine, begin, target in zip(chosen, begins, targets):
        shift = jnp.where(mine & (block >= begin), target - begin, shift)
    return block + shift


def lane_mean(x):
    return jnp.sum(x, axis=-1, keepdims=True) * (1.0 / HD)


def normalize(x):
    centred = x - lane_mean(x)
    inverse = lax.rsqrt(lane_mean(centred * centred) + EPS)
    return centred * inverse, inverse


def norm_back(grad, normed, inverse, gain):
    scaled = grad * gain
    first = lane_mean(scaled)
    second = lane_mean(scaled * normed)
    return inverse * (scaled - first - normed * second)


def dot(a, b, dims):
    return lax.dot_general(a, b, (dims, ((), ())), preferred_element_type=F32)


def kernel(
    n_dp, n_t, heads,
    q_hbm, k_hbm, v_hbm, cot_hbm, qg_hbm, kg_hbm, cnt_hbm, own_hbm, off_hbm,
    attn, gq_out, gk_out, gv_out,
    q_in, k_in, v_in, qg, kg, cnt, own, off,
    qn, kn, qh, kh, qi, ki, w_s, bias,
    sout, cat, lsend, rsend, pack,
    cown, ccat, lret, rret, csrc,
    in_sem, tab_sem, local_sem, a_send, a_recv, b_send, b_recv, d_send, d_recv,
):
    me_d = lax.axis_index("dp")
    me_t = lax.axis_index("tensor")
    left = lax.rem(me_d + n_dp - 1, n_dp)
    right = lax.rem(me_d + 1, n_dp)
    width = heads * HD
    blocks_t = OWN_BLOCKS // n_t
    peers = [lax.rem(me_t + s, n_t) for s in range(1, n_t)]

    loads = [
        pltpu.make_async_copy(src, dst, in_sem.at[i])
        for i, (src, dst) in enumerate(
            [(q_hbm, q_in), (k_hbm, k_in), (v_hbm, v_in), (qg_hbm, qg), (kg_hbm, kg)]
        )
    ]
    tables = [
        pltpu.make_async_copy(src, dst, tab_sem.at[i])
        for i, (src, dst) in enumerate([(cnt_hbm, cnt), (own_hbm, own), (off_hbm, off)])
    ]
    for copy in tables + loads:
        copy.start()

    barrier = pltpu.get_barrier_semaphore()
    for peer in peers:
        pl.semaphore_signal(barrier, inc=1, device_id={"tensor": peer}, device_id_type=MESH)
    for peer in (left, right):
        pl.semaphore_signal(barrier, inc=1, device_id={"dp": peer}, device_id_type=MESH)
    pl.semaphore_wait(barrier, n_t + 1)

    def cols(index):
        return pl.ds(pl.multiple_of(index * width, width), width)

    def token_blocks(index):
        return pl.ds(index * blocks_t, blocks_t)

    cot_copies = [
        pltpu.make_async_remote_copy(
            src_ref=cot_hbm.at[:, :, cols(peer)], dst_ref=cown.at[token_blocks(me_t)],
            send_sem=a_send.at[i], recv_sem=a_recv.at[i],
            device_id={"tensor": peer}, device_id_type=MESH,
        )
        for i, peer in enumerate(peers)
    ]
    for copy in cot_copies:
        copy.start()
    cot_local = pltpu.make_async_copy(
        cot_hbm.at[:, :, cols(me_t)], cown.at[token_blocks(me_t)], local_sem.at[0]
    )
    cot_local.start()

    for copy in tables:
        copy.wait()

    def entries(source):
        counts = [cnt[j, source] >> 4 for j in range(ENTRIES)]
        owners = [own[j, source] for j in range(ENTRIES)]
        offsets = [off[j, source] >> 4 for j in range(ENTRIES)]
        return counts, owners, offsets

    counts, owners, offsets = entries(me_d)
    l_counts, l_owners, l_offsets = entries(left)
    r_counts, r_owners, r_offsets = entries(right)
    starts, ends, total = [], [], jnp.int32(0)
    for count in counts:
        starts.append(total)
        total = total + count
        ends.append(total)
    to_left, left_begins = begins_of(counts, owners, left)
    to_right, right_begins = begins_of(counts, owners, right)
    from_left, fl_begins = begins_of(l_counts, l_owners, me_d)
    from_right, fr_begins = begins_of(r_counts, r_owners, me_d)

    key_row = lax.broadcasted_iota(jnp.int32, (SRC_ROWS, 1), 0)
    key_seg = jnp.zeros((SRC_ROWS, 1), jnp.int32)
    for end in ends:
        key_seg = key_seg + (key_row >= end * BLOCK).astype(jnp.int32)
    for i in range(TILES):
        query_row = lax.broadcasted_iota(jnp.int32, (1, TILE), 1) + i * TILE
        query_seg = jnp.zeros((1, TILE), jnp.int32)
        for end in ends:
            query_seg = query_seg + (query_row >= end * BLOCK).astype(jnp.int32)
        bias[i] = jnp.where(key_seg == query_seg, 0.0, -1e30).astype(F32)

    for copy in loads:
        copy.wait()

    scale = HD ** -0.5

    def forward(h, carry):
        lanes = pl.ds(pl.multiple_of(h * HD, HD), HD)
        query_hat, query_inv = normalize(q_in[:, lanes].astype(F32))
        key_hat, key_inv = normalize(k_in[:, lanes].astype(F32))
        qh[h] = query_hat
        kh[h] = key_hat
        qi[h] = query_inv
        ki[h] = key_inv
        qn[h] = (query_hat * qg[...]).astype(BF16)
        kn[h] = (key_hat * kg[...]).astype(BF16)
        value = v_in[:, lanes]
        for i in range(TILES):
            rows = pl.ds(i * TILE, TILE)
            scores = dot(kn[h], qn[h, rows, :], ((1,), (1,))) * scale + bias[i]
            powers = jnp.exp(scores - jnp.max(scores, axis=0, keepdims=True))
            weights = powers * (1.0 / jnp.sum(powers, axis=0, keepdims=True))
            w_s[h, i] = weights
            out = dot(weights.astype(BF16), value, ((0,), (0,))).astype(BF16)
            out = out.reshape(TILE_BLOCKS, BLOCK, HD)
            blocks = pl.ds(i * TILE_BLOCKS, TILE_BLOCKS)
            sout[blocks, :, lanes] = out
            cat[blocks, :, lanes] = out
        return carry

    lax.fori_loop(0, heads, forward, 0)

    def gather(dst, block, src, index):
        dst[block] = src[jnp.clip(index, 0, src.shape[0] - 1)]

    for block in range(CAP_BLOCKS):
        gather(lsend, block, sout, slot_source(to_left, left_begins, starts, block))
        gather(rsend, block, sout, slot_source(to_right, right_begins, starts, block))

    def exchange(to_l, to_r, dst, base, first):
        return [
            pltpu.make_async_remote_copy(
                src_ref=to_l, dst_ref=dst.at[pl.ds(base + CAP_BLOCKS, CAP_BLOCKS)],
                send_sem=d_send.at[first], recv_sem=d_recv.at[first],
                device_id={"dp": left}, device_id_type=MESH,
            ),
            pltpu.make_async_remote_copy(
                src_ref=to_r, dst_ref=dst.at[pl.ds(base, CAP_BLOCKS)],
                send_sem=d_send.at[first + 1], recv_sem=d_recv.at[first + 1],
                device_id={"dp": right}, device_id_type=MESH,
            ),
        ]

    out_moves = exchange(lsend, rsend, cat, SRC_BLOCKS, 0)
    for copy in out_moves:
        copy.start()
    for copy in out_moves:
        copy.wait()

    for block in range(OWN_BLOCKS):
        shift = jnp.int32(0)
        for j in range(ENTRIES):
            for mine, base, offset, count in (
                (owners[j] == me_d, starts[j], offsets[j], counts[j]),
                (from_left[j], SRC_BLOCKS + fl_begins[j], l_offsets[j], l_counts[j]),
                (from_right[j], SRC_BLOCKS + CAP_BLOCKS + fr_begins[j], r_offsets[j], r_counts[j]),
            ):
                inside = mine & (offset <= block) & (block < offset + count)
                shift = jnp.where(inside, base - offset, shift)
        gather(pack, block, cat, block + shift)

    out_copies = [
        pltpu.make_async_remote_copy(
            src_ref=pack.at[token_blocks(peer)], dst_ref=attn.at[:, :, cols(me_t)],
            send_sem=b_send.at[i], recv_sem=b_recv.at[i],
            device_id={"tensor": peer}, device_id_type=MESH,
        )
        for i, peer in enumerate(peers)
    ]
    for copy in out_copies:
        copy.start()
    out_local = pltpu.make_async_copy(
        pack.at[token_blocks(me_t)], attn.at[:, :, cols(me_t)], local_sem.at[1]
    )
    out_local.start()

    cot_local.wait()
    for copy in cot_copies:
        copy.wait()
    for block in range(CAP_BLOCKS):
        gather(lret, block, cown, slot_source(from_left, fl_begins, l_offsets, block))
        gather(rret, block, cown, slot_source(from_right, fr_begins, r_offsets, block))
    cot_moves = exchange(lret, rret, ccat, OWN_BLOCKS, 2)
    for copy in cot_moves:
        copy.start()
    ccat[pl.ds(0, OWN_BLOCKS)] = cown[...]
    for copy in cot_moves:
        copy.wait()
    for block in range(SRC_BLOCKS):
        shift = jnp.int32(0)
        for j in range(ENTRIES):
            base = jnp.where(
                owners[j] == me_d,
                offsets[j],
                jnp.where(to_left[j], OWN_BLOCKS + left_begins[j], OWN_BLOCKS + CAP_BLOCKS + right_begins[j]),
            )
            shift = jnp.where(block >= starts[j], base - starts[j], shift)
        gather(csrc, block, ccat, block + shift)

    in_use = key_row < total * BLOCK

    def backward(h, carry):
        lanes = pl.ds(pl.multiple_of(h * HD, HD), HD)
        value = v_in[:, lanes]
        grad_v = jnp.zeros((SRC_ROWS, HD), F32)
        grad_k = jnp.zeros((SRC_ROWS, HD), F32)
        grad_q = []
        for i in range(TILES):
            rows = pl.ds(i * TILE, TILE)
            cot = csrc[pl.ds(i * TILE_BLOCKS, TILE_BLOCKS), :, lanes].reshape(TILE, HD)
            weights = w_s[h, i]
            grad_w = dot(value, cot, ((1,), (1,)))
            inner = jnp.sum(weights * grad_w, axis=0, keepdims=True)
            grad_s = (weights * (grad_w - inner) * scale).astype(BF16)
            grad_v = grad_v + dot(weights.astype(BF16), cot, ((1,), (0,)))
            grad_k = grad_k + dot(grad_s, qn[h, rows, :], ((1,), (0,)))
            grad_q.append(dot(grad_s, kn[h], ((0,), (0,))))
        grad_q = norm_back(jnp.concatenate(grad_q, axis=0), qh[h], qi[h], qg[...])
        grad_k = norm_back(grad_k, kh[h], ki[h], kg[...])
        gq_out[:, lanes] = jnp.where(in_use, grad_q, 0.0).astype(BF16)
        gk_out[:, lanes] = jnp.where(in_use, grad_k, 0.0).astype(BF16)
        gv_out[:, lanes] = jnp.where(in_use, grad_v, 0.0).astype(BF16)
        return carry

    lax.fori_loop(0, heads, backward, 0)

    out_local.wait()
    for copy in out_copies:
        copy.wait()


def store_kernel(a, b, c, d, a_out, b_out, c_out, d_out, sem):
    copies = [
        pltpu.make_async_copy(src, dst, sem.at[i])
        for i, (src, dst) in enumerate(((a, a_out), (b, b_out), (c, c_out), (d, d_out)))
    ]
    for copy in copies:
        copy.start()
    for copy in copies:
        copy.wait()


def per_device(queries, keys_in, values, q_gain, k_gain, cotangent, patch_counts, image_owner, pack_offset):
    n_dp, n_t = lax.axis_size("dp"), lax.axis_size("tensor")
    width = queries.shape[1]
    heads = width // HD
    grad_shape = queries.shape
    attn_shape = (cotangent.shape[0] // BLOCK, BLOCK, cotangent.shape[1])
    dma = pltpu.SemaphoreType.DMA
    vmem = pltpu.VMEM

    def blocks(count):
        return vmem((count, BLOCK, width), BF16)

    scratch = [
        vmem((SRC_ROWS, width), BF16), vmem((SRC_ROWS, width), BF16), vmem((SRC_ROWS, width), BF16),
        vmem((1, HD), F32), vmem((1, HD), F32),
        pltpu.SMEM((ENTRIES, n_dp), jnp.int32),
        pltpu.SMEM((ENTRIES, n_dp), jnp.int32),
        pltpu.SMEM((ENTRIES, n_dp), jnp.int32),
        vmem((heads, SRC_ROWS, HD), BF16), vmem((heads, SRC_ROWS, HD), BF16),
        vmem((heads, SRC_ROWS, HD), F32), vmem((heads, SRC_ROWS, HD), F32),
        vmem((heads, SRC_ROWS, 1), F32), vmem((heads, SRC_ROWS, 1), F32),
        vmem((heads, TILES, SRC_ROWS, TILE), F32),
        vmem((TILES, SRC_ROWS, TILE), F32),
        blocks(SRC_BLOCKS), blocks(SRC_BLOCKS + 2 * CAP_BLOCKS),
        blocks(CAP_BLOCKS), blocks(CAP_BLOCKS), blocks(OWN_BLOCKS),
        blocks(OWN_BLOCKS), blocks(OWN_BLOCKS + 2 * CAP_BLOCKS),
        blocks(CAP_BLOCKS), blocks(CAP_BLOCKS), blocks(SRC_BLOCKS),
        dma((5,)), dma((3,)), dma((2,)),
        dma((n_t - 1,)), dma((n_t - 1,)), dma((n_t - 1,)), dma((n_t - 1,)), dma((4,)), dma((4,)),
    ]
    any_spec = pl.BlockSpec(memory_space=pl.ANY)
    vmem_spec = pl.BlockSpec(memory_space=pltpu.VMEM)
    flops = 12 * heads * SRC_ROWS * SRC_ROWS * HD
    operands = (
        queries, keys_in, values, cotangent.reshape(attn_shape), q_gain.reshape(1, HD), k_gain.reshape(1, HD),
        patch_counts.T, image_owner.T, pack_offset.T,
    )
    held = pl.pallas_call(
        functools.partial(kernel, n_dp, n_t, heads),
        out_shape=[vmem(attn_shape, BF16)] + [vmem(grad_shape, BF16)] * 3,
        in_specs=[any_spec] * 9,
        out_specs=[vmem_spec] * 4,
        scratch_shapes=scratch,
        compiler_params=pltpu.CompilerParams(
            collective_id=0, has_side_effects=True, vmem_limit_bytes=40 * 2**20
        ),
        cost_estimate=pl.CostEstimate(flops=flops, bytes_accessed=5 * 2**20, transcendentals=0),
    )(*[pltpu.with_memory_space_constraint(x, pltpu.HBM) for x in operands])
    held = [pltpu.with_memory_space_constraint(x, pltpu.VMEM) for x in held]
    attn_out, grad_q, grad_k, grad_v = pl.pallas_call(
        store_kernel,
        out_shape=[jax.ShapeDtypeStruct(x.shape, BF16) for x in held],
        in_specs=[vmem_spec] * 4,
        out_specs=[any_spec] * 4,
        scratch_shapes=[dma((4,))],
        compiler_params=pltpu.CompilerParams(vmem_limit_bytes=16 * 2**20),
        cost_estimate=pl.CostEstimate(flops=0, bytes_accessed=5 * 2**20, transcendentals=0),
    )(*held)
    return attn_out.reshape(cotangent.shape), grad_q, grad_k, grad_v


def solution(mesh):
    in_specs = (
        P("dp", "tensor"),
        P("dp", "tensor"),
        P("dp", "tensor"),
        P(),
        P(),
        P(("dp", "tensor"), None),
        P(),
        P(),
        P(),
    )
    out_specs = (P(("dp", "tensor"), None), P("dp", "tensor"), P("dp", "tensor"), P("dp", "tensor"))
    return jax.shard_map(
        per_device, mesh=mesh, in_specs=in_specs, out_specs=out_specs, check_vma=False
    )
```

time: 166 us -> 43.9 us (0.26)
  the two profiles are of different devices: /device:TPU:8 before, /device:TPU:32 now
where the time goes in v1:
time: 43.9 us; the launch traced here: 43.7 us
  Pallas kernels  43.1 us (98%)
  between operations  0.64 us (1%)
    pallas_call x1, Pallas kernels, per_device(): pl.pallas_call(functools.partial(kernel, n_dp, n_t, heads), out_shape=[vm...  41.6 us
    pallas_call x1, Pallas kernels, per_device(): pl.pallas_call(store_kernel, out_shape=[jax.ShapeDtypeStruct(x.shape, BF1...  1.47 us

profile of v1, /device:TPU:32, one launch (start us, length us, event | category | flops | bytes accessed | tf_op | source)
XLA Modules:
  0.0 43.7 jit_solution(1582807220853193907)
XLA Ops:
  0.6 41.6 %shard_map.120 = (bf16[2,16,6144]{2,1,0:T(8,128)(2,1)S(1)}, bf16[448,768]{1,0:T(8,128)(2,1)S(1)}, bf16[448,768]{1,0:T(8,128)(2,1)S(1)}, bf16[448,768]{1,0:T(8,128)(2,1)S(1)}) custom-call(bf16[448,768]{1,0:T(8,128)(2,1)} %q_hbm.1, bf16[448,768]{1,0:T(8,128)(2,1)} %k_hbm.1, bf16[448,768]{1,0:T(8,128)(2,1)} %v_hbm.1, bf16[2,16,6144]{2,1,0:T(8,128)(2,1)} %bitcast.7, ...), custom_call_target="tpu_custom_call" | custom-call | flops 1849688064 | bytes 5242880 | tf_op jit(solution)/shard_map/pallas_call | solution.py:345
  42.3 1.5 %shard_map.121 = (bf16[2,16,6144]{2,1,0:T(8,128)(2,1)}, bf16[448,768]{1,0:T(8,128)(2,1)}, bf16[448,768]{1,0:T(8,128)(2,1)}, bf16[448,768]{1,0:T(8,128)(2,1)}) custom-call(bf16[2,16,6144]{2,1,0:T(8,128)(2,1)S(1)} %get-tuple-element.12.a, bf16[448,768]{1,0:T(8,128)(2,1)S(1)} %get-tuple-element.13.b, bf16[448,768]{1,0:T(8,128)(2,1)S(1)} %get-tuple-element.14.c, ...), custom_call_target="tpu_custom_call" | custom-call | bytes 5242880 | tf_op jit(solution)/shard_map/pallas_call | solution.py:357

commit v2 on v1

v2 whole, which is shorter than its diff:
```python
import functools

import jax
import jax.numpy as jnp
from jax import lax
from jax.experimental import pallas as pl
from jax.experimental.pallas import tpu as pltpu
from jax.sharding import PartitionSpec as P

MESH = pl.DeviceIdType.MESH
HD = 128
OWN_ROWS = 256
CAP = 96
SRC_ROWS = 448
ENTRIES = 6
BLOCK = 16
OWN_BLOCKS = OWN_ROWS // BLOCK
CAP_BLOCKS = CAP // BLOCK
SRC_BLOCKS = SRC_ROWS // BLOCK
CHUNKS = (3, 3)
LOG2E = 1.4426950408889634
EPS = 1e-06
BF16 = jnp.bfloat16
F32 = jnp.float32


def begins_of(counts, owners, wanted):
    begins, total = [], jnp.int32(0)
    chosen = [owner == wanted for owner in owners]
    for count, mine in zip(counts, chosen):
        begins.append(total)
        total = total + jnp.where(mine, count, 0)
    return chosen, begins


def slot_source(chosen, begins, targets, block):
    shift = jnp.int32(0)
    for mine, begin, target in zip(chosen, begins, targets):
        shift = jnp.where(mine & (block >= begin), target - begin, shift)
    return block + shift


def lane_mean(x):
    return jnp.sum(x, axis=-1, keepdims=True) * (1.0 / HD)


def normalize(x):
    centred = x - lane_mean(x)
    inverse = lax.rsqrt(lane_mean(centred * centred) + EPS)
    return centred * inverse, inverse


def norm_back(grad, normed, inverse, gain):
    scaled = grad * gain
    first = lane_mean(scaled)
    second = lane_mean(scaled * normed)
    return inverse * (scaled - first - normed * second)


def dot(a, b, dims):
    return lax.dot_general(a, b, (dims, ((), ())), preferred_element_type=F32)


def kernel(n_dp, n_t, heads, *refs):
    (q_hbm, k_hbm, v_hbm, cot_hbm, qg_hbm, kg_hbm, cnt_hbm, own_hbm, off_hbm) = refs[:9]
    attn, gq_out, gk_out, gv_out = refs[9:13]
    (q_in, k_in, v_in, qg, kg, cnt, own, off, qn, kn, qh, kh, qi, ki, w_s, bias) = refs[13:29]
    in_sem, tab_sem, local_sem, a_send, a_recv, b_send, b_recv, d_send, d_recv, ready = refs[29:39]
    parts = [refs[39 + 10 * c: 49 + 10 * c] for c in range(len(CHUNKS))]
    firsts = [sum(CHUNKS[:c]) for c in range(len(CHUNKS))]

    me_d = lax.axis_index("dp")
    me_t = lax.axis_index("tensor")
    left = lax.rem(me_d + n_dp - 1, n_dp)
    right = lax.rem(me_d + 1, n_dp)
    width = heads * HD
    blocks_t = OWN_BLOCKS // n_t
    steps = sorted(range(1, n_t), key=lambda s: (-min(s, n_t - s), s))
    peers = [lax.rem(me_t + s, n_t) for s in steps]

    tables = [
        pltpu.make_async_copy(src, dst, tab_sem.at[i])
        for i, (src, dst) in enumerate([(cnt_hbm, cnt), (own_hbm, own), (off_hbm, off)])
    ]
    loads = [
        pltpu.make_async_copy(src, dst, in_sem.at[i])
        for i, (src, dst) in enumerate(
            [(q_hbm, q_in), (k_hbm, k_in), (v_hbm, v_in), (qg_hbm, qg), (kg_hbm, kg)]
        )
    ]
    barrier = pltpu.get_barrier_semaphore()
    for peer in peers:
        pl.semaphore_signal(barrier, inc=1, device_id={"tensor": peer}, device_id_type=MESH)
    pl.semaphore_signal(barrier, inc=1, device_id={"dp": left}, device_id_type=MESH)
    for copy in tables + loads:
        copy.start()
    pl.semaphore_wait(barrier, n_t)
    pl.semaphore_signal(ready, inc=1, device_id={"dp": right}, device_id_type=MESH)

    def cols(index, c):
        return pl.ds(pl.multiple_of(index * width + firsts[c] * HD, HD), CHUNKS[c] * HD)

    def token_blocks(index):
        return pl.ds(index * blocks_t, blocks_t)

    cot_copies, out_copies, cot_local, out_local = [], [], [], []
    for c, part in enumerate(parts):
        pack, cown = part[4], part[5]
        cot_copies.append([
            pltpu.make_async_remote_copy(
                src_ref=cot_hbm.at[:, :, cols(peer, c)], dst_ref=cown.at[token_blocks(me_t)],
                send_sem=a_send.at[c, i], recv_sem=a_recv.at[c, i],
                device_id={"tensor": peer}, device_id_type=MESH,
            )
            for i, peer in enumerate(peers)
        ])
        cot_local.append(pltpu.make_async_copy(
            cot_hbm.at[:, :, cols(me_t, c)], cown.at[token_blocks(me_t)], local_sem.at[0, c]
        ))
        out_copies.append([
            pltpu.make_async_remote_copy(
                src_ref=pack.at[token_blocks(peer)], dst_ref=attn.at[:, :, cols(me_t, c)],
                send_sem=b_send.at[c, i], recv_sem=b_recv.at[c, i],
                device_id={"tensor": peer}, device_id_type=MESH,
            )
            for i, peer in enumerate(peers)
        ])
        out_local.append(pltpu.make_async_copy(
            pack.at[token_blocks(me_t)], attn.at[:, :, cols(me_t, c)], local_sem.at[1, c]
        ))
    for c in range(len(CHUNKS)):
        for copy in cot_copies[c]:
            copy.start()
        cot_local[c].start()

    for copy in tables:
        copy.wait()

    def entries(source):
        counts = [cnt[j, source] >> 4 for j in range(ENTRIES)]
        owners = [own[j, source] for j in range(ENTRIES)]
        offsets = [off[j, source] >> 4 for j in range(ENTRIES)]
        return counts, owners, offsets

    counts, owners, offsets = entries(me_d)
    l_counts, l_owners, l_offsets = entries(left)
    r_counts, r_owners, r_offsets = entries(right)
    starts, ends, total = [], [], jnp.int32(0)
    for count in counts:
        starts.append(total)
        total = total + count
        ends.append(total)
    to_left, left_begins = begins_of(counts, owners, left)
    to_right, right_begins = begins_of(counts, owners, right)
    from_left, fl_begins = begins_of(l_counts, l_owners, me_d)
    from_right, fr_begins = begins_of(r_counts, r_owners, me_d)

    def segments(axis):
        row = lax.broadcasted_iota(jnp.int32, (SRC_ROWS, 1) if axis == 0 else (1, SRC_ROWS), axis)
        segment = jnp.zeros(row.shape, jnp.int32)
        for end in ends:
            segment = segment + (row >= end * BLOCK).astype(jnp.int32)
        return segment

    bias[...] = jnp.where(segments(0) == segments(1), 0.0, -1e30).astype(F32)
    in_use = lax.broadcasted_iota(jnp.int32, (SRC_ROWS, 1), 0) < total * BLOCK

    for copy in loads:
        copy.wait()

    scale = HD ** -0.5

    def forward(c):
        sout, cat = parts[c][0], parts[c][1]
        for h in range(firsts[c], firsts[c] + CHUNKS[c]):
            lanes = pl.ds(h * HD, HD)
            query_hat, query_inv = normalize(q_in[:, lanes].astype(F32))
            key_hat, key_inv = normalize(k_in[:, lanes].astype(F32))
            qh[h] = query_hat
            kh[h] = key_hat
            qi[h] = jnp.broadcast_to(query_inv, (SRC_ROWS, HD))
            ki[h] = jnp.broadcast_to(key_inv, (SRC_ROWS, HD))
            query_norm = (query_hat * qg[...]).astype(BF16)
            key_norm = (key_hat * kg[...]).astype(BF16)
            qn[h] = query_norm
            kn[h] = key_norm
            scores = dot(key_norm, query_norm, ((1,), (1,))) + bias[...]
            powers = jnp.exp2((scores - jnp.max(scores, axis=0, keepdims=True)) * (scale * LOG2E))
            weights = powers * (1.0 / jnp.sum(powers, axis=0, keepdims=True))
            w_s[h] = weights
            out = dot(weights.astype(BF16), v_in[:, lanes], ((0,), (0,))).astype(BF16)
            out = out.reshape(SRC_BLOCKS, BLOCK, HD)
            local = pl.ds((h - firsts[c]) * HD, HD)
            sout[:, :, local] = out
            cat[pl.ds(0, SRC_BLOCKS), :, local] = out

    def backward(c):
        csrc = parts[c][9]
        for h in range(firsts[c], firsts[c] + CHUNKS[c]):
            lanes = pl.ds(h * HD, HD)
            cot = csrc[:, :, pl.ds((h - firsts[c]) * HD, HD)].reshape(SRC_ROWS, HD)
            weights = w_s[h]
            grad_w = dot(v_in[:, lanes], cot, ((1,), (1,)))
            inner = jnp.sum(weights * grad_w, axis=0, keepdims=True)
            grad_s = (weights * (grad_w - inner) * scale).astype(BF16)
            grad_v = dot(weights.astype(BF16), cot, ((1,), (0,)))
            grad_k = dot(grad_s, qn[h], ((1,), (0,)))
            grad_q = dot(grad_s, kn[h], ((0,), (0,)))
            grad_q = norm_back(grad_q, qh[h], qi[h], qg[...])
            grad_k = norm_back(grad_k, kh[h], ki[h], kg[...])
            gq_out[:, lanes] = jnp.where(in_use, grad_q, 0.0).astype(BF16)
            gk_out[:, lanes] = jnp.where(in_use, grad_k, 0.0).astype(BF16)
            gv_out[:, lanes] = jnp.where(in_use, grad_v, 0.0).astype(BF16)

    def gather(dst, block, src, index):
        dst[block] = src[jnp.clip(index, 0, src.shape[0] - 1)]

    def exchange(to_l, to_r, dst, base, first, c):
        return [
            pltpu.make_async_remote_copy(
                src_ref=to_l, dst_ref=dst.at[pl.ds(base + CAP_BLOCKS, CAP_BLOCKS)],
                send_sem=d_send.at[first, c], recv_sem=d_recv.at[first, c],
                device_id={"dp": left}, device_id_type=MESH,
            ),
            pltpu.make_async_remote_copy(
                src_ref=to_r, dst_ref=dst.at[pl.ds(base, CAP_BLOCKS)],
                send_sem=d_send.at[first + 1, c], recv_sem=d_recv.at[first + 1, c],
                device_id={"dp": right}, device_id_type=MESH,
            ),
        ]

    out_moves = [exchange(p[2], p[3], p[1], SRC_BLOCKS, 0, c) for c, p in enumerate(parts)]
    cot_moves = [exchange(p[7], p[8], p[6], OWN_BLOCKS, 2, c) for c, p in enumerate(parts)]

    left_send = [slot_source(to_left, left_begins, starts, b) for b in range(CAP_BLOCKS)]
    right_send = [slot_source(to_right, right_begins, starts, b) for b in range(CAP_BLOCKS)]
    for c, part in enumerate(parts):
        sout, lsend, rsend = part[0], part[2], part[3]
        forward(c)
        for block in range(CAP_BLOCKS):
            gather(rsend, block, sout, right_send[block])
        out_moves[c][1].start()
        for block in range(CAP_BLOCKS):
            gather(lsend, block, sout, left_send[block])
        if c == 0:
            pl.semaphore_wait(ready, 1)
        out_moves[c][0].start()

    pack_from = []
    for block in range(OWN_BLOCKS):
        shift = jnp.int32(0)
        for j in range(ENTRIES):
            for mine, base, offset, count in (
                (owners[j] == me_d, starts[j], offsets[j], counts[j]),
                (from_left[j], SRC_BLOCKS + fl_begins[j], l_offsets[j], l_counts[j]),
                (from_right[j], SRC_BLOCKS + CAP_BLOCKS + fr_begins[j], r_offsets[j], r_counts[j]),
            ):
                inside = mine & (offset <= block) & (block < offset + count)
                shift = jnp.where(inside, base - offset, shift)
        pack_from.append(block + shift)
    left_back = [slot_source(from_left, fl_begins, l_offsets, b) for b in range(CAP_BLOCKS)]
    right_back = [slot_source(from_right, fr_begins, r_offsets, b) for b in range(CAP_BLOCKS)]

    for c, part in enumerate(parts):
        cat, pack, cown, ccat, lret, rret = part[1], part[4], part[5], part[6], part[7], part[8]
        cot_local[c].wait()
        for copy in cot_copies[c]:
            copy.wait_recv()
        for block in range(CAP_BLOCKS):
            gather(rret, block, cown, right_back[block])
            gather(lret, block, cown, left_back[block])
        for copy in cot_moves[c]:
            copy.start()
        for copy in out_moves[c]:
            copy.wait_recv()
        for block in range(OWN_BLOCKS):
            gather(pack, block, cat, pack_from[block])
        for copy in out_copies[c]:
            copy.start()
        out_local[c].start()
        ccat[pl.ds(0, OWN_BLOCKS)] = cown[...]

    cot_from = []
    for block in range(SRC_BLOCKS):
        shift = jnp.int32(0)
        for j in range(ENTRIES):
            base = jnp.where(
                owners[j] == me_d,
                offsets[j],
                jnp.where(to_left[j], OWN_BLOCKS + left_begins[j], OWN_BLOCKS + CAP_BLOCKS + right_begins[j]),
            )
            shift = jnp.where(block >= starts[j], base - starts[j], shift)
        cot_from.append(block + shift)
    for c, part in enumerate(parts):
        ccat, csrc = part[6], part[9]
        for copy in cot_moves[c]:
            copy.wait_recv()
        for block in range(SRC_BLOCKS):
            gather(csrc, block, ccat, cot_from[block])
        backward(c)

    for c in range(len(CHUNKS)):
        for copy in cot_copies[c] + out_moves[c] + cot_moves[c] + out_copies[c]:
            copy.wait_send()
        for copy in out_copies[c]:
            copy.wait_recv()
        out_local[c].wait()


def store_kernel(a, b, c, d, a_out, b_out, c_out, d_out, sem):
    copies = [
        pltpu.make_async_copy(src, dst, sem.at[i])
        for i, (src, dst) in enumerate(((a, a_out), (b, b_out), (c, c_out), (d, d_out)))
    ]
    for copy in copies:
        copy.start()
    for copy in copies:
        copy.wait()


def per_device(queries, keys_in, values, q_gain, k_gain, cotangent, patch_counts, image_owner, pack_offset):
    n_dp, n_t = lax.axis_size("dp"), lax.axis_size("tensor")
    width = queries.shape[1]
    heads = width // HD
    grad_shape = queries.shape
    attn_shape = (cotangent.shape[0] // BLOCK, BLOCK, cotangent.shape[1])
    dma = pltpu.SemaphoreType.DMA
    n_c = len(CHUNKS)
    vmem = pltpu.VMEM

    def blocks(count, run):
        return vmem((count, BLOCK, run * HD), BF16)

    scratch = [
        vmem((SRC_ROWS, width), BF16), vmem((SRC_ROWS, width), BF16), vmem((SRC_ROWS, width), BF16),
        vmem((1, HD), F32), vmem((1, HD), F32),
        pltpu.SMEM((ENTRIES, n_dp), jnp.int32),
        pltpu.SMEM((ENTRIES, n_dp), jnp.int32),
        pltpu.SMEM((ENTRIES, n_dp), jnp.int32),
        vmem((heads, SRC_ROWS, HD), BF16), vmem((heads, SRC_ROWS, HD), BF16),
        vmem((heads, SRC_ROWS, HD), F32), vmem((heads, SRC_ROWS, HD), F32),
        vmem((heads, SRC_ROWS, HD), F32), vmem((heads, SRC_ROWS, HD), F32),
        vmem((heads, SRC_ROWS, SRC_ROWS), F32),
        vmem((SRC_ROWS, SRC_ROWS), F32),
        dma((5,)), dma((3,)), dma((2, n_c)),
        dma((n_c, n_t - 1)), dma((n_c, n_t - 1)), dma((n_c, n_t - 1)), dma((n_c, n_t - 1)),
        dma((4, n_c)), dma((4, n_c)), pltpu.SemaphoreType.REGULAR,
    ]
    for run in CHUNKS:
        scratch += [
            blocks(SRC_BLOCKS, run), blocks(SRC_BLOCKS + 2 * CAP_BLOCKS, run),
            blocks(CAP_BLOCKS, run), blocks(CAP_BLOCKS, run), blocks(OWN_BLOCKS, run),
            blocks(OWN_BLOCKS, run), blocks(OWN_BLOCKS + 2 * CAP_BLOCKS, run),
            blocks(CAP_BLOCKS, run), blocks(CAP_BLOCKS, run), blocks(SRC_BLOCKS, run),
        ]
    any_spec = pl.BlockSpec(memory_space=pl.ANY)
    vmem_spec = pl.BlockSpec(memory_space=pltpu.VMEM)
    flops = 12 * heads * SRC_ROWS * SRC_ROWS * HD
    operands = (
        queries, keys_in, values, cotangent.reshape(attn_shape), q_gain.reshape(1, HD), k_gain.reshape(1, HD),
        patch_counts.T, image_owner.T, pack_offset.T,
    )
    held = pl.pallas_call(
        functools.partial(kernel, n_dp, n_t, heads),
        out_shape=[vmem(attn_shape, BF16)] + [vmem(grad_shape, BF16)] * 3,
        in_specs=[any_spec] * 9,
        out_specs=[vmem_spec] * 4,
        scratch_shapes=scratch,
        compiler_params=pltpu.CompilerParams(
            collective_id=0, has_side_effects=True, vmem_limit_bytes=40 * 2**20
        ),
        cost_estimate=pl.CostEstimate(flops=flops, bytes_accessed=5 * 2**20, transcendentals=0),
    )(*[pltpu.with_memory_space_constraint(x, pltpu.HBM) for x in operands])
    held = [pltpu.with_memory_space_constraint(x, pltpu.VMEM) for x in held]
    attn_out, grad_q, grad_k, grad_v = pl.pallas_call(
        store_kernel,
        out_shape=[jax.ShapeDtypeStruct(x.shape, BF16) for x in held],
        in_specs=[vmem_spec] * 4,
        out_specs=[any_spec] * 4,
        scratch_shapes=[dma((4,))],
        compiler_params=pltpu.CompilerParams(vmem_limit_bytes=16 * 2**20),
        cost_estimate=pl.CostEstimate(flops=0, bytes_accessed=5 * 2**20, transcendentals=0),
    )(*held)
    return attn_out.reshape(cotangent.shape), grad_q, grad_k, grad_v


def solution(mesh):
    in_specs = (
        P("dp", "tensor"),
        P("dp", "tensor"),
        P("dp", "tensor"),
        P(),
        P(),
        P(("dp", "tensor"), None),
        P(),
        P(),
        P(),
    )
    out_specs = (P(("dp", "tensor"), None), P("dp", "tensor"), P("dp", "tensor"), P("dp", "tensor"))
    return jax.shard_map(
        per_device, mesh=mesh, in_specs=in_specs, out_specs=out_specs, check_vma=False
    )
```

time: 43.9 us -> 33.8 us (0.77)
  the two profiles are of different devices: /device:TPU:32 before, /device:TPU:8 now
where the time goes in v2:
time: 33.8 us; the launch traced here: 33.4 us
  Pallas kernels  32.8 us (97%)
  between operations  0.64 us (2%)
    pallas_call x1, Pallas kernels, per_device(): pl.pallas_call(functools.partial(kernel, n_dp, n_t, heads), out_shape=[vm...  31.3 us
    pallas_call x1, Pallas kernels, per_device(): pl.pallas_call(store_kernel, out_shape=[jax.ShapeDtypeStruct(x.shape, BF1...  1.47 us

profile of v2, /device:TPU:8, one launch (start us, length us, event | category | flops | bytes accessed | tf_op | source)
XLA Modules:
  0.0 33.4 jit_solution(4008005649869810261)
XLA Ops:
  0.6 31.3 %shard_map.120 = (bf16[2,16,6144]{2,1,0:T(8,128)(2,1)S(1)}, bf16[448,768]{1,0:T(8,128)(2,1)S(1)}, bf16[448,768]{1,0:T(8,128)(2,1)S(1)}, bf16[448,768]{1,0:T(8,128)(2,1)S(1)}) custom-call(bf16[448,768]{1,0:T(8,128)(2,1)} %refs_0_.1, bf16[448,768]{1,0:T(8,128)(2,1)} %refs_1_.1, bf16[448,768]{1,0:T(8,128)(2,1)} %refs_2_.1, bf16[2,16,6144]{2,1,0:T(8,128)(2,1)} %bitcast.7, ...), custom_call_target="tpu_custom_call" | custom-call | flops 1849688064 | bytes 5242880 | tf_op jit(solution)/shard_map/pallas_call | solution.py:363
  31.9 1.5 %shard_map.121 = (bf16[2,16,6144]{2,1,0:T(8,128)(2,1)}, bf16[448,768]{1,0:T(8,128)(2,1)}, bf16[448,768]{1,0:T(8,128)(2,1)}, bf16[448,768]{1,0:T(8,128)(2,1)}) custom-call(bf16[2,16,6144]{2,1,0:T(8,128)(2,1)S(1)} %get-tuple-element.12.a, bf16[448,768]{1,0:T(8,128)(2,1)S(1)} %get-tuple-element.13.b, bf16[448,768]{1,0:T(8,128)(2,1)S(1)} %get-tuple-element.14.c, ...), custom_call_target="tpu_custom_call" | custom-call | bytes 5242880 | tf_op jit(solution)/shard_map/pallas_call | solution.py:375

commit v3 on v2

--- a/solution.py
+++ b/solution.py
@@ -17,7 +17,7 @@
 OWN_BLOCKS = OWN_ROWS // BLOCK
 CAP_BLOCKS = CAP // BLOCK
 SRC_BLOCKS = SRC_ROWS // BLOCK
-CHUNKS = (3, 3)
+CHUNKS = (2, 2, 2)
 LOG2E = 1.4426950408889634
 EPS = 1e-06
 BF16 = jnp.bfloat16
@@ -128,9 +128,14 @@
         out_local.append(pltpu.make_async_copy(
             pack.at[token_blocks(me_t)], attn.at[:, :, cols(me_t, c)], local_sem.at[1, c]
         ))
+    def send_cot():
+        for c in range(len(CHUNKS)):
+            for copy in cot_copies[c]:
+                copy.start()
+
+    odd = lax.rem(me_d, 2) == 1
+    pl.when(odd)(send_cot)
     for c in range(len(CHUNKS)):
-        for copy in cot_copies[c]:
-            copy.start()
         cot_local[c].start()
 
     for copy in tables:
@@ -237,14 +242,19 @@
     for c, part in enumerate(parts):
         sout, lsend, rsend = part[0], part[2], part[3]
         forward(c)
+        if c == 1:
+            pl.when(jnp.logical_not(odd))(send_cot)
         for block in range(CAP_BLOCKS):
             gather(rsend, block, sout, right_send[block])
         out_moves[c][1].start()
         for block in range(CAP_BLOCKS):
             gather(lsend, block, sout, left_send[block])
-        if c == 0:
+        if c == 1:
             pl.semaphore_wait(ready, 1)
-        out_moves[c][0].start()
+            for move in out_moves[:c]:
+                move[0].start()
+        if c >= 1:
+            out_moves[c][0].start()
 
     pack_from = []
     for block in range(OWN_BLOCKS):

time: 33.8 us -> 32.3 us (0.956)
  Pallas kernels: 32.8 us -> 31.5 us
    pallas_call x1, Pallas kernels: 31.3 us -> 30 us  [per_device(): pl.pallas_call(functools.partial(kernel, n_dp, n_t, heads), out_shape=[vm...]
where the time goes in v3:
time: 32.3 us; the launch traced here: 32.2 us
  Pallas kernels  31.5 us (98%)
  between operations  0.64 us (2%)
    pallas_call x1, Pallas kernels, per_device(): pl.pallas_call(functools.partial(kernel, n_dp, n_t, heads), out_shape=[vm...  30 us
    pallas_call x1, Pallas kernels, per_device(): pl.pallas_call(store_kernel, out_shape=[jax.ShapeDtypeStruct(x.shape, BF1...  1.47 us

profile of v3, /device:TPU:8, one launch (start us, length us, event | category | flops | bytes accessed | tf_op | source)
XLA Modules:
  0.0 32.2 jit_solution(838477725162836879)
XLA Ops:
  0.6 30.0 %shard_map.120 = (bf16[2,16,6144]{2,1,0:T(8,128)(2,1)S(1)}, bf16[448,768]{1,0:T(8,128)(2,1)S(1)}, bf16[448,768]{1,0:T(8,128)(2,1)S(1)}, bf16[448,768]{1,0:T(8,128)(2,1)S(1)}) custom-call(bf16[448,768]{1,0:T(8,128)(2,1)} %refs_0_.1, bf16[448,768]{1,0:T(8,128)(2,1)} %refs_1_.1, bf16[448,768]{1,0:T(8,128)(2,1)} %refs_2_.1, bf16[2,16,6144]{2,1,0:T(8,128)(2,1)} %bitcast.7, ...), custom_call_target="tpu_custom_call" | custom-call | flops 1849688064 | bytes 5242880 | tf_op jit(solution)/shard_map/pallas_call | solution.py:373
  30.7 1.5 %shard_map.121 = (bf16[2,16,6144]{2,1,0:T(8,128)(2,1)}, bf16[448,768]{1,0:T(8,128)(2,1)}, bf16[448,768]{1,0:T(8,128)(2,1)}, bf16[448,768]{1,0:T(8,128)(2,1)}) custom-call(bf16[2,16,6144]{2,1,0:T(8,128)(2,1)S(1)} %get-tuple-element.12.a, bf16[448,768]{1,0:T(8,128)(2,1)S(1)} %get-tuple-element.13.b, bf16[448,768]{1,0:T(8,128)(2,1)S(1)} %get-tuple-element.14.c, ...), custom_call_target="tpu_custom_call" | custom-call | bytes 5242880 | tf_op jit(solution)/shard_map/pallas_call | solution.py:385

commit v4 on v3

--- a/solution.py
+++ b/solution.py
@@ -94,8 +94,6 @@
     pl.semaphore_signal(barrier, inc=1, device_id={"dp": left}, device_id_type=MESH)
     for copy in tables + loads:
         copy.start()
-    pl.semaphore_wait(barrier, n_t)
-    pl.semaphore_signal(ready, inc=1, device_id={"dp": right}, device_id_type=MESH)
 
     def cols(index, c):
         return pl.ds(pl.multiple_of(index * width + firsts[c] * HD, HD), CHUNKS[c] * HD)
@@ -128,16 +126,6 @@
         out_local.append(pltpu.make_async_copy(
             pack.at[token_blocks(me_t)], attn.at[:, :, cols(me_t, c)], local_sem.at[1, c]
         ))
-    def send_cot():
-        for c in range(len(CHUNKS)):
-            for copy in cot_copies[c]:
-                copy.start()
-
-    odd = lax.rem(me_d, 2) == 1
-    pl.when(odd)(send_cot)
-    for c in range(len(CHUNKS)):
-        cot_local[c].start()
-
     for copy in tables:
         copy.wait()
 
@@ -169,6 +157,19 @@
 
     bias[...] = jnp.where(segments(0) == segments(1), 0.0, -1e30).astype(F32)
     in_use = lax.broadcasted_iota(jnp.int32, (SRC_ROWS, 1), 0) < total * BLOCK
+
+    pl.semaphore_wait(barrier, n_t)
+    pl.semaphore_signal(ready, inc=1, device_id={"dp": right}, device_id_type=MESH)
+
+    def send_cot():
+        for c in range(len(CHUNKS)):
+            for copy in cot_copies[c]:
+                copy.start()
+
+    odd = lax.rem(me_d, 2) == 1
+    pl.when(odd)(send_cot)
+    for c in range(len(CHUNKS)):
+        cot_local[c].start()
 
     for copy in loads:
         copy.wait()

time: 32.3 us -> 31.9 us (0.988)
  Pallas kernels: 31.5 us -> 31.1 us
    pallas_call x1, Pallas kernels: 30 us -> 29.7 us  [per_device(): pl.pallas_call(functools.partial(kernel, n_dp, n_t, heads), out_shape=[vm...]
where the time goes in v4:
time: 31.9 us; the launch traced here: 31.8 us
  Pallas kernels  31.1 us (97%)
  between operations  0.64 us (2%)
    pallas_call x1, Pallas kernels, per_device(): pl.pallas_call(functools.partial(kernel, n_dp, n_t, heads), out_shape=[vm...  29.7 us
    pallas_call x1, Pallas kernels, per_device(): pl.pallas_call(store_kernel, out_shape=[jax.ShapeDtypeStruct(x.shape, BF1...  1.47 us

profile of v4, /device:TPU:8, one launch (start us, length us, event | category | flops | bytes accessed | tf_op | source)
XLA Modules:
  0.0 31.8 jit_solution(15767636624250523359)
XLA Ops:
  0.6 29.7 %shard_map.120 = (bf16[2,16,6144]{2,1,0:T(8,128)(2,1)S(1)}, bf16[448,768]{1,0:T(8,128)(2,1)S(1)}, bf16[448,768]{1,0:T(8,128)(2,1)S(1)}, bf16[448,768]{1,0:T(8,128)(2,1)S(1)}) custom-call(bf16[448,768]{1,0:T(8,128)(2,1)} %refs_0_.1, bf16[448,768]{1,0:T(8,128)(2,1)} %refs_1_.1, bf16[448,768]{1,0:T(8,128)(2,1)} %refs_2_.1, bf16[2,16,6144]{2,1,0:T(8,128)(2,1)} %bitcast.7, ...), custom_call_target="tpu_custom_call" | custom-call | flops 1849688064 | bytes 5242880 | tf_op jit(solution)/shard_map/pallas_call | solution.py:374
  30.3 1.5 %shard_map.121 = (bf16[2,16,6144]{2,1,0:T(8,128)(2,1)}, bf16[448,768]{1,0:T(8,128)(2,1)}, bf16[448,768]{1,0:T(8,128)(2,1)}, bf16[448,768]{1,0:T(8,128)(2,1)}) custom-call(bf16[2,16,6144]{2,1,0:T(8,128)(2,1)S(1)} %get-tuple-element.12.a, bf16[448,768]{1,0:T(8,128)(2,1)S(1)} %get-tuple-element.13.b, bf16[448,768]{1,0:T(8,128)(2,1)S(1)} %get-tuple-element.14.c, ...), custom_call_target="tpu_custom_call" | custom-call | bytes 5242880 | tf_op jit(solution)/shard_map/pallas_call | solution.py:386
